TPU v7x, 128 devices: a whole 4x4x4 slice. The times are simulated.
128 devices in a mesh: sec: 2 (over core), dev: 64 (over z, x, y).
Axes of the slice: x: 4, y: 4, z: 4, core: 2. Of those that a mesh axis runs over, the one named last changes fastest.
Arguments:
- hidden_state: bfloat16 [4096, 2048], P(('sec', 'dev')), may hold values from -6 to 6
- queries: bfloat16 [4096, 2048], P(('sec', 'dev')), may hold values from -7 to 7
- new_keys: bfloat16 [4096, 256], P(('sec', 'dev')), may hold values from -4 to 4
- new_values: bfloat16 [4096, 256], P(('sec', 'dev')), may hold values from -6 to 6
- cache_keys: bfloat16 [4096, 96, 256], P(('sec', 'dev')), may hold values from -7 to 7
- cache_values: bfloat16 [4096, 96, 256], P(('sec', 'dev')), may hold values from -6 to 6
- lengths: int32 [4096], P(('sec', 'dev')), may hold values from 2 to 96, as said below
- o_weight: bfloat16 [2048, 2048], replicated, may hold values from -0.125 to 0.125
- norm_gain: float32 [2048], replicated, may hold values from 0.1 to 1.9
- expert_ids: int32 [4096, 8], P(('sec', 'dev')), may hold values from 0 to 127, all different within a row; in each aligned block of 16 rows (0 to 15, 16 to 31, ...) at most 2 rows name the same one
- gate_values: float32 [4096, 8], P(('sec', 'dev')), may hold values from 0.05 to 1
- w_gate: bfloat16 [128, 2048, 768], P(('sec', 'dev')), may hold values from -0.125 to 0.125
- w_up: bfloat16 [128, 2048, 768], P(('sec', 'dev')), may hold values from -0.125 to 0.125
- w_down: bfloat16 [128, 768, 2048], P(('sec', 'dev')), may hold values from -0.21875 to 0.21875
Outputs:
- new_hidden: bfloat16 [4096, 2048], P(('sec', 'dev'))
Inputs may be any that keep to these rules, and one draw needn't show every extreme that they name: `lengths`: every row has at least 2 live positions, and some row has 96. `expert_ids`: within each aligned block of 16 rows (one micro-batch of one device) no expert is named by more than 2 rows; in some blocks one expert is named by exactly 2.
All inputs are finite; a program needn't handle non-finite values.
Results may differ from a plain program's by a relative error of at most 0.02.
Values may be sent and summed in bfloat16 or wider, within the bound.
No kernel may reach another device: no remote copies, remote signals or barrier semaphores. Data moves between devices by JAX's collectives and lax.ppermute only.
A program may use at most 128 MiB of HBM per device.

v0:
```python
import jax
import jax.numpy as jnp
from jax import lax
from jax.sharding import PartitionSpec as P

D = 2048
HEADS = 16
KV_HEADS = 2
HEAD_DIM = 128
GROUP = 8
TOP = 8
MICRO = 16
LMAX = 96


def attend(query_rows, new_key_rows, new_value_rows, key_rows, value_rows, length_rows):
    row_count = query_rows.shape[0]
    score_scale = HEAD_DIM ** (-0.5)
    query_heads = query_rows.reshape(row_count, KV_HEADS, GROUP, HEAD_DIM)
    key_heads = key_rows.reshape(row_count, LMAX, KV_HEADS, HEAD_DIM)
    value_heads = value_rows.reshape(row_count, LMAX, KV_HEADS, HEAD_DIM)
    scores = (
        jnp.einsum("rkgd,rlkd->rkgl", query_heads, key_heads, preferred_element_type=jnp.float32)
        * score_scale
    )
    live_mask = jnp.arange(LMAX, dtype=jnp.int32)[None, :] < length_rows[:, None]
    scores = jnp.where(live_mask[:, None, None, :], scores, -jnp.inf)
    own_key = new_key_rows.reshape(row_count, KV_HEADS, HEAD_DIM)
    own_score = (
        jnp.einsum("rkgd,rkd->rkg", query_heads, own_key, preferred_element_type=jnp.float32)
        * score_scale
    )
    peak = jnp.maximum(jnp.max(scores, axis=-1), own_score)
    weights_raw = jnp.exp(scores - peak[..., None])
    weight_own = jnp.exp(own_score - peak)
    denominator = jnp.sum(weights_raw, axis=-1) + weight_own
    attn_probs = (weights_raw / denominator[..., None]).astype(jnp.bfloat16)
    probs_own = (weight_own / denominator).astype(jnp.bfloat16)
    own_value = new_value_rows.reshape(row_count, KV_HEADS, 1, HEAD_DIM).astype(jnp.float32)
    attn_out = jnp.einsum(
        "rkgl,rlkd->rkgd", attn_probs, value_heads, preferred_element_type=jnp.float32
    )
    attn_out = attn_out + probs_own.astype(jnp.float32)[..., None] * own_value
    return attn_out.reshape(row_count, HEADS * HEAD_DIM).astype(jnp.bfloat16)


def settle(hidden_rows, attended, o_weight, norm_gain):
    after_attn = (
        hidden_rows.astype(jnp.float32)
        + jnp.dot(attended, o_weight, preferred_element_type=jnp.float32)
    ).astype(jnp.bfloat16)
    after_float = after_attn.astype(jnp.float32)
    normed = (
        after_float
        * lax.rsqrt(jnp.mean(after_float * after_float, axis=-1, keepdims=True) + 1e-06)
        * norm_gain
    ).astype(jnp.bfloat16)
    return (after_float, normed)


def experts_apply(received, w_gate, w_up, w_down):
    gate_part = jnp.einsum("sjmd,jdf->sjmf", received, w_gate, preferred_element_type=jnp.float32)
    up_part = jnp.einsum("sjmd,jdf->sjmf", received, w_up, preferred_element_type=jnp.float32)
    hidden_act = (jax.nn.silu(gate_part) * up_part).astype(jnp.bfloat16)
    return jnp.einsum(
        "sjmf,jfd->sjmd", hidden_act, w_down, preferred_element_type=jnp.float32
    ).astype(jnp.bfloat16)


def route(normed, ids, gates, w_gate, w_up, w_down, capacity):
    sec_count = lax.axis_size("sec")
    dev_count = lax.axis_size("dev")
    device_count = sec_count * dev_count
    local_count = w_gate.shape[0]
    expert_count = device_count * local_count
    row_count = ids.shape[0]
    flat_ids = ids.reshape(-1)
    onehot = (flat_ids[:, None] == jnp.arange(expert_count, dtype=jnp.int32)[None, :]).astype(
        jnp.int32
    )
    earlier = jnp.cumsum(onehot, axis=0) - onehot
    slot_index = jnp.sum(earlier * onehot, axis=1)
    target_slot = flat_ids * capacity + slot_index
    source_rows = jnp.arange(row_count * TOP, dtype=jnp.int32) // TOP
    outgoing = (
        jnp.zeros((expert_count * capacity, D), jnp.bfloat16)
        .at[target_slot]
        .set(normed[source_rows])
    )
    returned = lax.all_to_all(
        experts_apply(
            lax.all_to_all(
                outgoing.reshape(device_count, local_count, capacity, D),
                ("sec", "dev"),
                split_axis=0,
                concat_axis=0,
                tiled=True,
            ),
            w_gate,
            w_up,
            w_down,
        ),
        ("sec", "dev"),
        split_axis=0,
        concat_axis=0,
        tiled=True,
    )
    picked = returned.reshape(expert_count * capacity, D)[target_slot].reshape(row_count, TOP, D)
    return jnp.sum(picked.astype(jnp.float32) * gates[:, :, None], axis=1)


def layer_rows(
    hidden_rows,
    query_rows,
    new_key_rows,
    new_value_rows,
    key_rows,
    value_rows,
    length_rows,
    o_weight,
    norm_gain,
    ids,
    gates,
    w_gate,
    w_up,
    w_down,
    capacity,
):
    attended = attend(query_rows, new_key_rows, new_value_rows, key_rows, value_rows, length_rows)
    after_float, normed = settle(hidden_rows, attended, o_weight, norm_gain)
    mixture = route(normed, ids, gates, w_gate, w_up, w_down, capacity)
    return (after_float + mixture).astype(jnp.bfloat16)


def on_device(
    hidden_state,
    queries,
    new_keys,
    new_values,
    cache_keys,
    cache_values,
    lengths,
    o_weight,
    norm_gain,
    expert_ids,
    gate_values,
    w_gate,
    w_up,
    w_down,
):
    device_count = lax.axis_size("sec") * lax.axis_size("dev")
    most_rows = max(2, 2 * MICRO * TOP // (w_gate.shape[0] * device_count))
    arrays = (hidden_state, queries, new_keys, new_values, cache_keys, cache_values, lengths)
    return layer_rows(
        *arrays, o_weight, norm_gain, expert_ids, gate_values, w_gate, w_up, w_down, 2 * most_rows
    )


def solution(mesh):
    return jax.shard_map(
        on_device,
        mesh=mesh,
        in_specs=(
            P(("sec", "dev"), None),
            P(("sec", "dev"), None),
            P(("sec", "dev"), None),
            P(("sec", "dev"), None),
            P(("sec", "dev"), None, None),
            P(("sec", "dev"), None, None),
            P(("sec", "dev")),
            P(),
            P(),
            P(("sec", "dev"), None),
            P(("sec", "dev"), None),
            P(("sec", "dev"), None, None),
            P(("sec", "dev"), None, None),
            P(("sec", "dev"), None, None),
        ),
        out_specs=P(("sec", "dev"), None),
        check_vma=False,
    )
```

profile of v0, /device:TPU:5, one launch (start us, length us, event | category | flops | bytes accessed | tf_op | source)
XLA Modules:
  0.0 147.7 jit_solution(8899139345775045122)
XLA Ops:
  0.0 0.0 copy-start
  0.0 0.9 copy.61
  0.9 0.6 eq.29
  1.5 0.7 eq.25
  2.2 1.3 broadcast_multiply_fusion
  3.5 0.6 compare_select_fusion
  4.0 0.9 copy.73
  5.0 0.7 iota_compare_fusion.1
  5.7 3.0 %fusion.72 = (f32[32,2,8]{2,1,0:T(2,128)}, f32[32,2,8,96]{3,2,1,0:T(8,128)S(1)}) fusion(bf16[32,2,8,128]{3,2,1,0:T(8,128)(2,1)S(1)} %bitcast.153, pred[32,96]{1,0:T(8,128)(4,1)S(1)} %iota_compare_fusion.1, bf16[32,96,256]{2,1,0:T(8,128)(2,1)} %param.18), kind=kOutput, calls=%fused_computation.80 | convolution fusion | flops 12729856 | bytes 1905664 | tf_op jit(solution)/shard_map/rkgd,rlkd->rkgl/dot_general | solution.py:23
  8.7 0.8 copy.54
  9.6 1.3 reshape.216
  10.9 1.6 %fusion.73 = f32[32,2,1,8]{3,2,1,0:T(1,128)} fusion(bf16[32,2,8,128]{3,2,1,0:T(8,128)(2,1)S(1)} %bitcast.154, bf16[32,2,128,1]{2,3,1,0:T(2,128)(2,1)} %reshape.216), kind=kOutput, calls=%fused_computation.81 | convolution fusion | flops 131072 | bytes 149504 | tf_op jit(solution)/shard_map/rkgd,rkd->rkg/dot_general | solution.py:30
  12.5 0.8 copy.70
  13.3 0.1 copy.55
  13.4 0.3 fusion.58
  13.7 0.1 copy.56
  13.8 0.1 copy.57
  13.9 0.1 copy.59
  14.0 0.7 reshape.184
  14.7 0.0 copy-start.2
  14.7 2.0 %fusion.47 = bf16[32,2,8,128]{3,2,1,0:T(8,128)(2,1)S(1)} fusion(f32[32,2,8,96]{3,2,1,0:T(8,128)S(1)} %get-tuple-element.8, f32[32,2,128]{2,1,0:T(2,128)S(1)} %reshape.184, f32[32,2,8]{2,1,0:T(2,128)S(1)} %copy.59, f32[32,2,8]{2,1,0:T(2,128)S(1)} %copy.57, f32[32,2,8]{2,1,0:T(2,128)S(1)} %copy.55, bf16[32,96,256]{2,1,0:T(8,128)(2,1)} %param.19), kind=kOutput, calls=%fused_computation.37 | convolution fusion | flops 12926976 | bytes 1939456 | tf_op jit(solution)/shard_map/rkgl,rlkd->rkgd/dot_general | solution.py:40
  16.8 0.0 copy-done.2
  16.8 0.0 copy-start.3
  16.8 5.0 %multiply_reduce_fusion = (f32[32]{0:T(128)S(1)}, f32[32,2048]{1,0:T(8,128)S(1)}) fusion(bf16[2048,2048]{1,0:T(8,128)(2,1)} %param.21, bf16[4,8,16,128]{3,2,1,0:T(8,128)(2,1)S(1)} %bitcast.155, bf16[32,2048]{1,0:T(8,128)(2,1)S(1)} %copy-done.2), kind=kOutput, calls=%fused_computation.44 | convolution fusion | flops 268828640 | bytes 8913024 | tf_op jit(solution)/shard_map/dot_general | solution.py:50
  21.8 0.6 add_rsqrt_fusion
  22.4 0.0 copy-done.3
  22.4 0.7 copy.63
  23.2 1.0 fusion.59
  24.3 0.7 copy.60
  25.1 0.7 mul.87
  25.7 0.6 pad_clamp_fusion.1
  26.3 0.8 fusion.63
  27.2 0.7 compare_select_fusion.1
  27.9 0.8 multiply_convert_fusion
  28.7 7.1 %scatter_custom_fusion = bf16[512,2048]{1,0:T(8,128)(2,1)} fusion(s32[256]{0:T(256)S(1)} %bitcast.159, bf16[32,2048]{1,0:T(8,128)(2,1)S(1)} %multiply_convert_fusion, s32[1024]{0:T(1024)S(1)} %pad_clamp_fusion.1, bf16[]{:T(256)} %constant.35.clone.1), kind=kCustom, calls=%fused_computation.38 | custom fusion | bytes 2097154 | tf_op jit(solution)/shard_map/scatter | solution.py:88
  35.7 4.1 %reshape.177 = bf16[128,1,4,2048]{3,2,0,1:T(4,128)(2,1)} reshape(bf16[512,2048]{1,0:T(8,128)(2,1)} %scatter_custom_fusion) | data formatting | bytes 4194304 | tf_op jit(solution)/shard_map/reshape | solution.py:93
  39.9 0.0 copy-start.5
  39.9 40.1 %all_to_all.10 = bf16[128,1,4,2048]{3,2,1,0:T(4,128)(2,1)S(1)} all-to-all(bf16[128,1,4,2048]{3,2,1,0:T(4,128)(2,1)} %bitcast.150), channel_id=1, replica_groups=mesh['sec'=2,'dev'=64] {'sec','dev'}, dimensions={0} | all-to-all | bytes 4194304 | tf_op jit(solution)/shard_map/all_to_all | solution.py:92
  80.0 0.0 copy-start.1
  80.0 1.3 copy-done.1
  81.3 0.0 copy-done.5
  81.3 4.8 %fusion.4 = f32[128,4,768]{2,0,1:T(8,128)} fusion(bf16[1,2048,768]{2,1,0:T(8,128)(2,1)S(1)} %copy-done.5, bf16[128,1,4,2048]{3,2,1,0:T(4,128)(2,1)S(1)} %all_to_all.10), kind=kOutput, calls=%fused_computation.7 | convolution fusion | flops 1610612736 | bytes 6815744 | tf_op jit(solution)/shard_map/sjmd,jdf->sjmf/dot_general | solution.py:62
  86.0 0.0 copy-done
  86.0 9.9 %fusion.9 = bf16[128,1,4,2048]{3,0,2,1:T(8,128)(2,1)} fusion(bf16[1,768,2048]{2,1,0:T(8,128)(2,1)S(1)} %copy-done, bf16[1,2048,768]{2,1,0:T(8,128)(2,1)} %param.26, bf16[128,1,4,2048]{3,2,1,0:T(4,128)(2,1)} %copy-done.1, f32[128,4,768]{2,0,1:T(8,128)} %fusion.4), kind=kOutput, calls=%fused_computation.10 | convolution fusion | flops 3224633344 | bytes 12058624 | tf_op jit(solution)/shard_map/sjmf,jfd->sjmd/dot_general | solution.py:65
  95.9 4.5 %copy.67 = bf16[128,1,4,2048]{3,2,1,0:T(4,128)(2,1)} copy(bf16[128,1,4,2048]{3,0,2,1:T(8,128)(2,1)} %fusion.9) | data formatting | bytes 4194304 | tf_op jit(solution)/shard_map/convert_element_type | solution.py:67
  100.4 0.0 copy-start.4
  100.4 6.3 %all-to-all-start.1 = ((bf16[128,1,4,2048]{3,2,1,0:T(4,128)(2,1)}), bf16[128,1,4,2048]{3,2,1,0:T(4,128)(2,1)}, u32[]{:S(2)}, u32[]{:S(2)}) async-start(bf16[128,1,4,2048]{3,2,1,0:T(4,128)(2,1)} %copy.67), calls=%async_computation.1 | async-start | bytes 4194304 | tf_op jit(solution)/shard_map/all_to_all | solution.py:90
  106.7 0.0 copy-done.4
  106.7 0.1 copy.68
  106.8 28.8 %all-to-all-done.1 = bf16[128,1,4,2048]{3,2,1,0:T(4,128)(2,1)} async-done(((bf16[128,1,4,2048]{3,2,1,0:T(4,128)(2,1)}), bf16[128,1,4,2048]{3,2,1,0:T(4,128)(2,1)}, u32[]{:S(2)}, u32[]{:S(2)}) %all-to-all-start.1) | async-done | bytes 2097184 | tf_op jit(solution)/shard_map/all_to_all | solution.py:90
  135.6 4.0 %reshape.183 = bf16[512,2048]{1,0:T(8,128)(2,1)} reshape(bf16[128,1,4,2048]{3,2,1,0:T(4,128)(2,1)} %all-to-all-done.1) | data formatting | bytes 4194304 | tf_op jit(solution)/shard_map/reshape | solution.py:108
  139.6 5.2 %gather_fusion = bf16[256,2048]{1,0:T(8,128)(2,1)} fusion(bf16[512,2048]{1,0:T(8,128)(2,1)} %reshape.183, s32[1024]{0:T(1024)S(1)} %pad_clamp_fusion), kind=kCustom, calls=%fused_computation.1 | custom fusion | bytes 2098176 | tf_op jit(solution)/shard_map/gather | solution.py:108
  144.8 2.2 %fusion.14 = f32[32,2048]{1,0:T(8,128)S(1)} fusion(bf16[256,2048]{1,0:T(8,128)(2,1)} %gather_fusion, f32[32,8]{1,0:T(8,128)S(1)} %copy.68), kind=kLoop, calls=%fused_computation.15 | loop fusion | flops 1507328 | bytes 1311744 | tf_op jit(solution)/shard_map/reduce_sum | solution.py:109
  147.0 0.7 add_convert_fusion
  (9 shorter events, 0.1 us)
Async XLA Ops:
  0.0 86.0 %copy-start = (bf16[1,768,2048]{2,1,0:T(8,128)(2,1)S(1)}, bf16[1,768,2048]{2,1,0:T(8,128)(2,1)}, u32[]{:S(2)}) copy-start(bf16[1,768,2048]{2,1,0:T(8,128)(2,1)} %param.27) | copy-start | bytes 9437188
  14.7 2.0 %copy-start.2 = (bf16[32,2048]{1,0:T(8,128)(2,1)S(1)}, bf16[32,2048]{1,0:T(8,128)(2,1)}, u32[]{:S(2)}) copy-start(bf16[32,2048]{1,0:T(8,128)(2,1)} %param.14) | copy-start | bytes 393220
  16.8 5.7 %copy-start.3 = (s32[2,128]{1,0:T(2,128)S(1)}, s32[2,128]{1,0:T(2,128)}, u32[]{:S(2)}) copy-start(s32[2,128]{1,0:T(2,128)} %eq.29) | copy-start | bytes 3076
  39.9 41.4 %copy-start.5 = (bf16[1,2048,768]{2,1,0:T(8,128)(2,1)S(1)}, bf16[1,2048,768]{2,1,0:T(8,128)(2,1)}, u32[]{:S(2)}) copy-start(bf16[1,2048,768]{2,1,0:T(8,128)(2,1)} %param.25) | copy-start | bytes 9437188
  80.0 1.3 copy-start.1
  100.4 6.3 %copy-start.4 = (f32[32,8]{0,1:T(8,128)S(1)}, f32[32,8]{0,1:T(8,128)}, u32[]{:S(2)}) copy-start(f32[32,8]{0,1:T(8,128)} %param.24) | copy-start | bytes 3076
  100.4 35.2 %all-to-all-start.1 = ((bf16[128,1,4,2048]{3,2,1,0:T(4,128)(2,1)}), bf16[128,1,4,2048]{3,2,1,0:T(4,128)(2,1)}, u32[]{:S(2)}, u32[]{:S(2)}) async-start(bf16[128,1,4,2048]{3,2,1,0:T(4,128)(2,1)} %copy.67), calls=%async_computation.1 | async-start | bytes 4194304 | tf_op jit(solution)/shard_map/all_to_all | solution.py:90
where the time goes:
time: 149 us; the launch traced here: 148 us
  blocking collectives  40.1 us (27%)
  local copies, waits for them, and re-layouts  35.6 us (24%)
  waiting for transfers between devices  28.8 us (19%)
  matrix products  26.3 us (18%)
  other arithmetic  10.4 us (7%)
  starting transfers between devices  6.27 us (4%)
    all_to_all x1, blocking collectives, route(): lax.all_to_all(outgoing.reshape(device_count, local_count, capacity, D),...  40.1 us
    all_to_all x1, waiting for transfers between devices, route(): lax.all_to_all(experts_apply(lax.all_to_all(outgoing.reshape(device_count...  28.8 us
    dot_general x1, matrix products, experts_apply(): jnp.einsum('sjmf,jfd->sjmd', hidden_act, w_down, preferred_element_type=j...  9.85 us
    scatter x1, local copies, waits for them, and re-layouts, route(): outgoing = jnp.zeros((expert_count * capacity, D), jnp.bfloat16).at[targe...  7.06 us
    all_to_all x1, starting transfers between devices, route(): lax.all_to_all(experts_apply(lax.all_to_all(outgoing.reshape(device_count...  6.27 us
    gather x1, local copies, waits for them, and re-layouts, route(): returned.reshape(expert_count * capacity, D)[target_slot]  5.21 us
    dot_general x1, matrix products, settle(): jnp.dot(attended, o_weight, preferred_element_type=jnp.float32)  5.04 us
    dot_general x1, matrix products, experts_apply(): jnp.einsum('sjmd,jdf->sjmf', received, w_gate, preferred_element_type=jnp...  4.77 us
  transfers between devices with their start and end apart: 1, of which 1 were waited for; matrix products, arithmetic and copies ran while one was open for 0% of the time, Pallas kernels for 0%

commit v1 on v0

v1 whole, which is shorter than its diff:
```python
import jax
import jax.numpy as jnp
from jax import lax
from jax.experimental import pallas as pl
from jax.experimental.pallas import tpu as pltpu
from jax.sharding import PartitionSpec as P

D = 2048
FF = 768
KV_HEADS = 2
HEAD_DIM = 128
GROUP = 8
TOP = 8
MICRO = 16
ROWS_DEV = 32
LMAX = 96
MOST = 2
EXPERTS = 128

SLOTS = MOST * ROWS_DEV // MICRO
CHUNK_ROWS = 16
CHUNK_COLS = SLOTS * D // CHUNK_ROWS
BLOCKS = CHUNK_ROWS // SLOTS
LINES = EXPERTS * CHUNK_ROWS
TALL = BLOCKS * ROWS_DEV

SUB = 8
GROUPS = ROWS_DEV // SUB
O_CHUNKS = 8
O_DEPTH = D // O_CHUNKS
O_STARTS = O_CHUNKS // GROUPS
WEIGHT_PARTS = 4
W_STARTS = 2
FF_CHUNK = 256

SHUFFLE = 256
SOURCES = SHUFFLE // CHUNK_ROWS
BAND = SOURCES * SLOTS
SHUFFLES = LINES // SHUFFLE

MIB = 2**20
F32 = jnp.float32
BF16 = jnp.bfloat16
NT = (((1,), (1,)), ((), ()))
VMEM = pl.BlockSpec(memory_space=pltpu.VMEM)
SMEM = pl.BlockSpec(memory_space=pltpu.SMEM)
HBM = pl.BlockSpec(memory_space=pltpu.HBM)


def iota(shape, dim):
    return lax.broadcasted_iota(jnp.int32, shape, dim)


def dot(a, b):
    return jnp.dot(a, b, preferred_element_type=F32)


def tile_lanes(array):
    return jnp.concatenate([array] * BLOCKS, axis=1)


def slot_table(ids):
    ids = tile_lanes(ids)
    expert = iota((EXPERTS, TALL), 0)
    named = jnp.zeros((EXPERTS, TALL), F32)
    for k in range(TOP):
        named = jnp.where(ids[k : k + 1, :] == expert, 1.0, named)
    first, second = iota((TALL, TALL), 0), iota((TALL, TALL), 1)
    before = jnp.where((first // MICRO == second // MICRO) & (first < second), 1.0, 0.0)
    earlier = dot(named.astype(BF16), before.astype(BF16))
    micro = (iota((EXPERTS, TALL), 1) % ROWS_DEV) // MICRO
    return named * (earlier + (micro * MOST + 1).astype(F32))


def attend_group(group, lengths_ref, queries, new_keys, new_values, keys, values, attended):
    scale = HEAD_DIM ** (-0.5)
    mine = pl.ds(group * SUB, SUB)
    query = queries[mine, :].astype(F32)
    own_key = new_keys[mine, :].astype(F32)
    own_value = new_values[mine, :].astype(F32)
    cache = pl.ds(group * SUB * LMAX, SUB * LMAX)
    row = iota((SUB, SUB * LMAX), 0)
    length = jnp.zeros((SUB, SUB * LMAX), jnp.int32)
    for r in range(SUB):
        length = jnp.where(row == r, lengths_ref[group * SUB + r], length)
    place = iota((SUB, SUB * LMAX), 1) - row * LMAX
    bias = jnp.where((place >= 0) & (place < length), 0.0, -jnp.inf)
    bias = jnp.concatenate([bias] * GROUP, axis=0)
    for kv in range(KV_HEADS):
        cols = slice(kv * HEAD_DIM, (kv + 1) * HEAD_DIM)
        first = kv * GROUP * HEAD_DIM
        heads = jnp.concatenate(
            [query[:, first + g * HEAD_DIM : first + (g + 1) * HEAD_DIM] for g in range(GROUP)],
            axis=0,
        )
        key_tall = jnp.concatenate([own_key[:, cols]] * GROUP, axis=0)
        value_tall = jnp.concatenate([own_value[:, cols]] * GROUP, axis=0)
        scores = lax.dot_general(
            heads.astype(BF16), keys[cache, cols], NT, preferred_element_type=F32
        )
        scores = scores * scale + bias
        own = jnp.sum(heads * key_tall, axis=1, keepdims=True) * scale
        peak = jnp.maximum(jnp.max(scores, axis=1, keepdims=True), own)
        raw = jnp.exp(scores - peak)
        raw_own = jnp.exp(own - peak)
        share = 1.0 / (jnp.sum(raw, axis=1, keepdims=True) + raw_own)
        probs = (raw * share).astype(BF16)
        probs_own = (raw_own * share).astype(BF16).astype(F32)
        result = dot(probs, values[cache, cols]) + probs_own * value_tall
        for g in range(GROUP):
            attended[mine, first + g * HEAD_DIM : first + (g + 1) * HEAD_DIM] = result[
                g * SUB : (g + 1) * SUB, :
            ]


def combine_weights(table, ids, gates):
    ids = tile_lanes(ids)
    gates = tile_lanes(gates)
    expert = iota((EXPERTS, TALL), 0)
    gate = jnp.zeros((EXPERTS, TALL), F32)
    for k in range(TOP):
        gate = jnp.where(ids[k : k + 1, :] == expert, gates[k : k + 1, :], gate)
    gate = jnp.transpose(gate)
    high = gate.astype(BF16)
    low = (gate - high.astype(F32)).astype(BF16)
    table = jnp.transpose(table).astype(BF16)
    lane = iota((EXPERTS, LINES), 1)
    spread = (lane // CHUNK_ROWS == iota((EXPERTS, LINES), 0)).astype(BF16)
    lane = iota((TALL, LINES), 1)
    wanted = jnp.where(
        (lane // SLOTS) % BLOCKS == iota((TALL, LINES), 0) // ROWS_DEV,
        (lane % SLOTS + 1).astype(F32),
        -1.0,
    )
    live = dot(table, spread) == wanted
    return [jnp.where(live, dot(part, spread), 0.0).astype(BF16) for part in (high, low)]


def dispatch_weights(table):
    line = iota((LINES, EXPERTS), 0)
    spread = (line // CHUNK_ROWS == iota((LINES, EXPERTS), 1)).astype(BF16)
    wanted = jnp.where(
        (line // SLOTS) % BLOCKS == iota((LINES, TALL), 1) // ROWS_DEV,
        (line % SLOTS + 1).astype(F32),
        -1.0,
    )
    return jnp.where(dot(spread, table.astype(BF16)) == wanted, 1.0, 0.0).astype(BF16)


def attention_kernel(
    lengths_ref,
    ids_ref,
    gates_ref,
    gain_ref,
    hidden_hbm,
    queries_hbm,
    new_keys_hbm,
    new_values_hbm,
    keys_hbm,
    values_hbm,
    o_hbm,
    gate_hbm,
    up_hbm,
    down_hbm,
    after_ref,
    outgoing_ref,
    mixing_ref,
    gate_ref,
    up_ref,
    down_ref,
    hidden,
    queries,
    new_keys,
    new_values,
    keys,
    values,
    o_weight,
    attended,
    dispatch,
    small_sem,
    key_sem,
    value_sem,
    o_sem,
    weight_sem,
):
    small = [
        pltpu.make_async_copy(queries_hbm, queries, small_sem.at[0]),
        pltpu.make_async_copy(new_keys_hbm, new_keys, small_sem.at[1]),
        pltpu.make_async_copy(new_values_hbm, new_values, small_sem.at[2]),
        pltpu.make_async_copy(hidden_hbm, hidden, small_sem.at[3]),
    ]
    for copy in small:
        copy.start()
    key_copies, value_copies, o_copies = [], [], []
    for group in range(GROUPS):
        part = pl.ds(group * SUB * LMAX, SUB * LMAX)
        key_copies.append(
            pltpu.make_async_copy(keys_hbm.at[part], keys.at[part], key_sem.at[group])
        )
        value_copies.append(
            pltpu.make_async_copy(values_hbm.at[part], values.at[part], value_sem.at[group])
        )
        key_copies[group].start()
        value_copies[group].start()
    for c in range(O_CHUNKS):
        part = pl.ds(c * O_DEPTH, O_DEPTH)
        o_copies.append(pltpu.make_async_copy(o_hbm.at[part], o_weight.at[part], o_sem.at[c]))
    weight_copies = []
    for i, (source, target) in enumerate(
        ((gate_hbm, gate_ref), (up_hbm, up_ref), (down_hbm, down_ref))
    ):
        depth = source.shape[0] // WEIGHT_PARTS
        for c in range(WEIGHT_PARTS):
            part = pl.ds(c * depth, depth)
            weight_copies.append(
                pltpu.make_async_copy(source.at[part], target.at[part], weight_sem.at[i, c])
            )

    table = slot_table(ids_ref[...])
    dispatch[...] = dispatch_weights(table)
    high, low = combine_weights(table, ids_ref[...], gates_ref[...])
    mixing_ref[:TALL, :] = high
    mixing_ref[TALL:, :] = low

    for copy in small:
        copy.wait()
    waiting = list(o_copies)
    for group in range(GROUPS):
        key_copies[group].wait()
        value_copies[group].wait()
        for copy in waiting[:O_STARTS]:
            copy.start()
        waiting = waiting[O_STARTS:]
        attend_group(group, lengths_ref, queries, new_keys, new_values, keys, values, attended)

    total = hidden[...].astype(F32)
    waiting = list(weight_copies)
    for c in range(O_CHUNKS):
        o_copies[c].wait()
        for copy in waiting[:W_STARTS]:
            copy.start()
        waiting = waiting[W_STARTS:]
        part = slice(c * O_DEPTH, (c + 1) * O_DEPTH)
        total = total + dot(attended[:, part].astype(BF16), o_weight[part, :])
    after = total.astype(BF16)
    after_ref[...] = after
    after = after.astype(F32)
    mean = jnp.mean(after * after, axis=1, keepdims=True)
    normed = (after * lax.rsqrt(mean + 1e-6) * gain_ref[...]).astype(BF16)
    stacked = jnp.concatenate(
        [normed[:, q * CHUNK_COLS : (q + 1) * CHUNK_COLS] for q in range(BLOCKS)], axis=0
    )
    outgoing_ref[...] = dot(dispatch[...], stacked).astype(BF16)
    for copy in weight_copies:
        copy.wait()


def attention_part(
    lengths,
    ids,
    gates,
    gain,
    hidden,
    queries,
    new_keys,
    new_values,
    keys,
    values,
    o_weight,
    w_gate,
    w_up,
    w_down,
):
    cache = (ROWS_DEV * LMAX, KV_HEADS * HEAD_DIM)
    return pl.pallas_call(
        attention_kernel,
        out_shape=(
            pltpu.VMEM((ROWS_DEV, D), BF16),
            pltpu.VMEM((LINES, CHUNK_COLS), BF16),
            pltpu.VMEM((2 * TALL, LINES), BF16),
            pltpu.VMEM((D, FF), BF16),
            pltpu.VMEM((D, FF), BF16),
            pltpu.VMEM((FF, D), BF16),
        ),
        in_specs=[SMEM] + [VMEM] * 3 + [HBM] * 10,
        out_specs=(VMEM,) * 6,
        scratch_shapes=[
            pltpu.VMEM((ROWS_DEV, D), BF16),
            pltpu.VMEM((ROWS_DEV, D), BF16),
            pltpu.VMEM((ROWS_DEV, KV_HEADS * HEAD_DIM), BF16),
            pltpu.VMEM((ROWS_DEV, KV_HEADS * HEAD_DIM), BF16),
            pltpu.VMEM(cache, BF16),
            pltpu.VMEM(cache, BF16),
            pltpu.VMEM((D, D), BF16),
            pltpu.VMEM((ROWS_DEV, D), F32),
            pltpu.VMEM((LINES, TALL), BF16),
            pltpu.SemaphoreType.DMA((4,)),
            pltpu.SemaphoreType.DMA((GROUPS,)),
            pltpu.SemaphoreType.DMA((GROUPS,)),
            pltpu.SemaphoreType.DMA((O_CHUNKS,)),
            pltpu.SemaphoreType.DMA((3, WEIGHT_PARTS)),
        ],
        compiler_params=pltpu.CompilerParams(vmem_limit_bytes=50 * MIB),
        cost_estimate=pl.CostEstimate(
            flops=2 * ROWS_DEV * D * D, bytes_accessed=16 * MIB, transcendentals=0
        ),
        name="attend",
    )(
        lengths,
        ids,
        gates,
        gain,
        hidden,
        queries,
        new_keys,
        new_values,
        keys,
        values,
        o_weight,
        w_gate,
        w_up,
        w_down,
    )


def shuffle_matrix(back):
    one, other = (1, 0) if back else (0, 1)
    banded = iota((SHUFFLE, SHUFFLE), one)
    chunked = iota((SHUFFLE, SHUFFLE), other)
    same = (
        (banded // BAND == (chunked // SLOTS) % BLOCKS)
        & ((banded % BAND) // SLOTS == chunked // CHUNK_ROWS)
        & (banded % SLOTS == chunked % SLOTS)
    )
    return same.astype(F32).astype(BF16)


def expert_kernel(received_ref, gate_ref, up_ref, down_ref, out_ref, rows, inner):
    spread = shuffle_matrix(False)
    for b in range(SHUFFLES):
        part = dot(spread, received_ref[b * SHUFFLE : (b + 1) * SHUFFLE, :]).astype(BF16)
        for q in range(BLOCKS):
            rows[b * BAND : (b + 1) * BAND, q * CHUNK_COLS : (q + 1) * CHUNK_COLS] = part[
                q * BAND : (q + 1) * BAND, :
            ]
    for f in range(0, FF, FF_CHUNK):
        gate = dot(rows[...], gate_ref[:, f : f + FF_CHUNK])
        up = dot(rows[...], up_ref[:, f : f + FF_CHUNK])
        inner[:, f : f + FF_CHUNK] = (gate / (1.0 + jnp.exp(-gate)) * up).astype(BF16)
    for q in range(BLOCKS):
        cols = slice(q * CHUNK_COLS, (q + 1) * CHUNK_COLS)
        rows[:, cols] = dot(inner[...], down_ref[:, cols]).astype(BF16)
    gather = shuffle_matrix(True)
    for b in range(SHUFFLES):
        part = jnp.concatenate(
            [
                rows[b * BAND : (b + 1) * BAND, q * CHUNK_COLS : (q + 1) * CHUNK_COLS]
                for q in range(BLOCKS)
            ],
            axis=0,
        )
        out_ref[b * SHUFFLE : (b + 1) * SHUFFLE, :] = dot(gather, part).astype(BF16)


def expert_part(received, w_gate, w_up, w_down):
    count = EXPERTS * SLOTS
    return pl.pallas_call(
        expert_kernel,
        out_shape=pltpu.VMEM((LINES, CHUNK_COLS), BF16),
        in_specs=[VMEM] * 4,
        out_specs=VMEM,
        scratch_shapes=[pltpu.VMEM((count, D), BF16), pltpu.VMEM((count, FF), BF16)],
        compiler_params=pltpu.CompilerParams(vmem_limit_bytes=32 * MIB),
        cost_estimate=pl.CostEstimate(
            flops=6 * count * D * FF, bytes_accessed=12 * MIB, transcendentals=0
        ),
        name="experts",
    )(received, w_gate, w_up, w_down)


def combine_kernel(returned_ref, mixing_ref, after_ref, out_ref):
    mix = dot(mixing_ref[...], returned_ref[...])
    mix = mix[:TALL] + mix[TALL:]
    for q in range(BLOCKS):
        cols = slice(q * CHUNK_COLS, (q + 1) * CHUNK_COLS)
        out_ref[:, cols] = (
            after_ref[:, cols].astype(F32) + mix[q * ROWS_DEV : (q + 1) * ROWS_DEV, :]
        ).astype(BF16)


def combine(returned, mixing, after):
    return pl.pallas_call(
        combine_kernel,
        out_shape=jax.ShapeDtypeStruct((ROWS_DEV, D), BF16),
        in_specs=[VMEM] * 3,
        out_specs=VMEM,
        compiler_params=pltpu.CompilerParams(vmem_limit_bytes=24 * MIB),
        cost_estimate=pl.CostEstimate(
            flops=4 * TALL * LINES * CHUNK_COLS, bytes_accessed=4 * MIB, transcendentals=0
        ),
        name="combine",
    )(returned, mixing, after)


def exchange(array):
    return lax.all_to_all(
        array.reshape(EXPERTS, CHUNK_ROWS, CHUNK_COLS),
        ("sec", "dev"),
        split_axis=0,
        concat_axis=0,
        tiled=True,
    ).reshape(LINES, CHUNK_COLS)


def on_device(
    hidden_state,
    queries,
    new_keys,
    new_values,
    cache_keys,
    cache_values,
    lengths,
    o_weight,
    norm_gain,
    expert_ids,
    gate_values,
    w_gate,
    w_up,
    w_down,
):
    after, outgoing, mixing, *weights = attention_part(
        lengths,
        expert_ids.T,
        gate_values.T,
        norm_gain.reshape(1, D),
        hidden_state,
        queries,
        new_keys,
        new_values,
        cache_keys.reshape(-1, KV_HEADS * HEAD_DIM),
        cache_values.reshape(-1, KV_HEADS * HEAD_DIM),
        o_weight,
        w_gate.reshape(D, FF),
        w_up.reshape(D, FF),
        w_down.reshape(FF, D),
    )
    made = expert_part(exchange(outgoing), *weights)
    return combine(exchange(made), mixing, after)


def solution(mesh):
    split = ("sec", "dev")
    rows = P(split, None)
    stack = P(split, None, None)
    return jax.shard_map(
        on_device,
        mesh=mesh,
        in_specs=(
            rows,
            rows,
            rows,
            rows,
            stack,
            stack,
            P(split),
            P(),
            P(),
            rows,
            rows,
            stack,
            stack,
            stack,
        ),
        out_specs=rows,
        check_vma=False,
    )
```

time: 149 us -> 93 us (0.62)
  local copies, waits for them, and re-layouts: 35.6 us -> 0 us
  blocking collectives: 40.1 us -> 74.8 us
  waiting for transfers between devices: 28.8 us -> 0 us
  matrix products: 26.3 us -> 0 us
  Pallas kernels: 0 us -> 17.9 us
  other arithmetic: 10.4 us -> 0 us
  starting transfers between devices: 6.27 us -> 0 us
    all_to_all x1 -> x2, blocking collectives: 40.1 us -> 74.8 us  [exchange(): lax.all_to_all(array.reshape(EXPERTS, CHUNK_ROWS, CHUNK_COLS), ('sec', 'd...]
    all_to_all x1 -> x0, waiting for transfers between devices: 28.8 us -> none  [route(): lax.all_to_all(experts_apply(lax.all_to_all(outgoing.reshape(device_count...]
    dot_general x6 -> x0, matrix products: 26.3 us -> none  [the longest x1 9.85 us: experts_apply(): jnp.einsum('sjmf,jfd->sjmd', hidden_act, w_down, preferred_element_type=j...]
    pallas_call x0 -> x3, Pallas kernels: none -> 17.9 us  [the longest x1 10.4 us: attention_part(): pl.pallas_call(attention_kernel, out_shape=(pltpu.VMEM((ROWS_DEV, D), BF1...]
    reshape x3 -> x0, local copies, waits for them, and re-layouts: 9.43 us -> none  [the longest x1 4.12 us: route(): outgoing.reshape(device_count, local_count, capacity, D)]
    scatter x1 -> x0, local copies, waits for them, and re-layouts: 7.06 us -> none  [route(): outgoing = jnp.zeros((expert_count * capacity, D), jnp.bfloat16).at[targe...]
    all_to_all x1 -> x0, starting transfers between devices: 6.27 us -> none  [route(): lax.all_to_all(experts_apply(lax.all_to_all(outgoing.reshape(device_count...]
    convert_element_type x3 -> x0, local copies, waits for them, and re-layouts: 5.33 us -> none  [the longest x1 4.5 us: experts_apply(): return jnp.einsum('sjmf,jfd->sjmd', hidden_act, w_down, preferred_element...]
  transfers between devices with their start and end apart: 1 -> 0, of which waited for: 1 -> 0; matrix products, arithmetic and copies ran while one was open for 0% -> 0% of each run, Pallas kernels for 0% -> 0%
where the time goes in v1:
time: 93 us; the launch traced here: 92.8 us
  blocking collectives  74.8 us (80%)
  Pallas kernels  17.9 us (19%)
    all_to_all x2, blocking collectives, exchange(): lax.all_to_all(array.reshape(EXPERTS, CHUNK_ROWS, CHUNK_COLS), ('sec', 'd...  74.8 us
    pallas_call x1, Pallas kernels, attention_part(): pl.pallas_call(attention_kernel, out_shape=(pltpu.VMEM((ROWS_DEV, D), BF1...  10.4 us
    pallas_call x1, Pallas kernels, expert_part(): pl.pallas_call(expert_kernel, out_shape=pltpu.VMEM((LINES, CHUNK_COLS), B...  6.18 us

profile of v1, /device:TPU:5, one launch (start us, length us, event | category | flops | bytes accessed | tf_op | source)
XLA Modules:
  0.0 92.8 jit_solution(15255864323320640384)
XLA Ops:
  0.0 10.4 %attend.1 = (bf16[32,2048]{1,0:T(8,128)(2,1)S(1)}, bf16[2048,512]{1,0:T(8,128)(2,1)S(1)}, bf16[256,2048]{1,0:T(8,128)(2,1)S(1)}, bf16[2048,768]{1,0:T(8,128)(2,1...) custom-call(s32[32]{0:T(128)} %lengths_ref.1, s32[8,32]{1,0:T(8,128)} %bitcast.22, f32[8,32]{1,0:T(8,128)} %bitcast.23, ...), custom_call_target="tpu_custom_call" | custom-call | flops 268435456 | bytes 16777216 | tf_op jit(solution)/shard_map/attend/pallas_call | solution.py:275
  10.4 39.9 %all_to_all.10 = bf16[128,16,512]{2,1,0:T(8,128)(2,1)S(1)} all-to-all(bf16[128,16,512]{2,1,0:T(8,128)(2,1)S(1)} %bitcast.13), channel_id=1, replica_groups=mesh['sec'=2,'dev'=64] {'sec','dev'}, dimensions={0} | all-to-all | bytes 4194304 | tf_op jit(solution)/shard_map/all_to_all | solution.py:406
  50.3 6.2 %experts.1 = bf16[2048,512]{1,0:T(8,128)(2,1)S(1)} custom-call(bf16[2048,512]{1,0:T(8,128)(2,1)S(1)} %bitcast.14, bf16[2048,768]{1,0:T(8,128)(2,1)S(1)} %get-tuple-element.12.gate_ref, bf16[2048,768]{1,0:T(8,128)(2,1)S(1)} %get-tuple-element.13.up_ref, bf16[768,2048]{1,0:T(8,128)(2,1)S(1)} %get-tuple-element.14.down_ref), custom_call_target="tpu_custom_call" | custom-call | flops 4831838208 | bytes 12582912 | tf_op jit(solution)/shard_map/experts/pallas_call | solution.py:367
  56.5 34.9 %all_to_all.11 = bf16[128,16,512]{2,1,0:T(8,128)(2,1)S(1)} all-to-all(bf16[128,16,512]{2,1,0:T(8,128)(2,1)S(1)} %bitcast.15), channel_id=1, replica_groups=mesh['sec'=2,'dev'=64] {'sec','dev'}, dimensions={0} | all-to-all | bytes 4194304 | tf_op jit(solution)/shard_map/all_to_all | solution.py:406
  91.4 1.4 %combine.1 = bf16[32,2048]{1,0:T(8,128)(2,1)} custom-call(bf16[2048,512]{1,0:T(8,128)(2,1)S(1)} %bitcast.12, bf16[256,2048]{1,0:T(8,128)(2,1)S(1)} %get-tuple-element.15.mixing_ref, bf16[32,2048]{1,0:T(8,128)(2,1)S(1)} %get-tuple-element.16.after_ref), custom_call_target="tpu_custom_call" | custom-call | flops 536870912 | bytes 4194304 | tf_op jit(solution)/shard_map/combine/pallas_call | solution.py:392

commit v2 on v1

--- a/solution.py
+++ b/solution.py
@@ -1,3 +1,5 @@
+import math
+
 import jax
 import jax.numpy as jnp
 from jax import lax
@@ -28,9 +30,7 @@
 GROUPS = ROWS_DEV // SUB
 O_CHUNKS = 8
 O_DEPTH = D // O_CHUNKS
-O_STARTS = O_CHUNKS // GROUPS
 WEIGHT_PARTS = 4
-W_STARTS = 2
 FF_CHUNK = 256
 
 SHUFFLE = 256
@@ -43,7 +43,6 @@
 BF16 = jnp.bfloat16
 NT = (((1,), (1,)), ((), ()))
 VMEM = pl.BlockSpec(memory_space=pltpu.VMEM)
-SMEM = pl.BlockSpec(memory_space=pltpu.SMEM)
 HBM = pl.BlockSpec(memory_space=pltpu.HBM)
 
 
@@ -72,8 +71,8 @@
     return named * (earlier + (micro * MOST + 1).astype(F32))
 
 
-def attend_group(group, lengths_ref, queries, new_keys, new_values, keys, values, attended):
-    scale = HEAD_DIM ** (-0.5)
+def attend_group(group, lengths, queries, new_keys, new_values, keys, values, attended):
+    scale = HEAD_DIM ** (-0.5) * math.log2(math.e)
     mine = pl.ds(group * SUB, SUB)
     query = queries[mine, :].astype(F32)
     own_key = new_keys[mine, :].astype(F32)
@@ -82,7 +81,7 @@
     row = iota((SUB, SUB * LMAX), 0)
     length = jnp.zeros((SUB, SUB * LMAX), jnp.int32)
     for r in range(SUB):
-        length = jnp.where(row == r, lengths_ref[group * SUB + r], length)
+        length = jnp.where(row == r, lengths[group * SUB + r], length)
     place = iota((SUB, SUB * LMAX), 1) - row * LMAX
     bias = jnp.where((place >= 0) & (place < length), 0.0, -jnp.inf)
     bias = jnp.concatenate([bias] * GROUP, axis=0)
@@ -98,15 +97,13 @@
         scores = lax.dot_general(
             heads.astype(BF16), keys[cache, cols], NT, preferred_element_type=F32
         )
-        scores = scores * scale + bias
-        own = jnp.sum(heads * key_tall, axis=1, keepdims=True) * scale
+        scores = scores + bias
+        own = jnp.sum(heads * key_tall, axis=1, keepdims=True)
         peak = jnp.maximum(jnp.max(scores, axis=1, keepdims=True), own)
-        raw = jnp.exp(scores - peak)
-        raw_own = jnp.exp(own - peak)
+        raw = jnp.exp2((scores - peak) * scale)
+        raw_own = jnp.exp2((own - peak) * scale)
         share = 1.0 / (jnp.sum(raw, axis=1, keepdims=True) + raw_own)
-        probs = (raw * share).astype(BF16)
-        probs_own = (raw_own * share).astype(BF16).astype(F32)
-        result = dot(probs, values[cache, cols]) + probs_own * value_tall
+        result = (dot(raw.astype(BF16), values[cache, cols]) + raw_own * value_tall) * share
         for g in range(GROUP):
             attended[mine, first + g * HEAD_DIM : first + (g + 1) * HEAD_DIM] = result[
                 g * SUB : (g + 1) * SUB, :
@@ -148,10 +145,10 @@
 
 
 def attention_kernel(
-    lengths_ref,
-    ids_ref,
-    gates_ref,
-    gain_ref,
+    lengths_hbm,
+    ids_hbm,
+    gates_hbm,
+    gain_hbm,
     hidden_hbm,
     queries_hbm,
     new_keys_hbm,
@@ -161,13 +158,15 @@
     o_hbm,
     gate_hbm,
     up_hbm,
-    down_hbm,
     after_ref,
     outgoing_ref,
     mixing_ref,
     gate_ref,
     up_ref,
-    down_ref,
+    lengths,
+    ids,
+    gates,
+    gain,
     hidden,
     queries,
     new_keys,
@@ -183,11 +182,19 @@
     o_sem,
     weight_sem,
 ):
+    pairs = (
+        (ids_hbm, ids),
+        (gates_hbm, gates),
+        (queries_hbm, queries),
+        (new_keys_hbm, new_keys),
+        (new_values_hbm, new_values),
+        (lengths_hbm, lengths),
+        (hidden_hbm, hidden),
+        (gain_hbm, gain),
+    )
     small = [
-        pltpu.make_async_copy(queries_hbm, queries, small_sem.at[0]),
-        pltpu.make_async_copy(new_keys_hbm, new_keys, small_sem.at[1]),
-        pltpu.make_async_copy(new_values_hbm, new_values, small_sem.at[2]),
-        pltpu.make_async_copy(hidden_hbm, hidden, small_sem.at[3]),
+        pltpu.make_async_copy(source, target, small_sem.at[i])
+        for i, (source, target) in enumerate(pairs)
     ]
     for copy in small:
         copy.start()
@@ -207,7 +214,7 @@
         o_copies.append(pltpu.make_async_copy(o_hbm.at[part], o_weight.at[part], o_sem.at[c]))
     weight_copies = []
     for i, (source, target) in enumerate(
-        ((gate_hbm, gate_ref), (up_hbm, up_ref), (down_hbm, down_ref))
+        ((gate_hbm, gate_ref), (up_hbm, up_ref))
     ):
         depth = source.shape[0] // WEIGHT_PARTS
         for c in range(WEIGHT_PARTS):
@@ -216,37 +223,35 @@
                 pltpu.make_async_copy(source.at[part], target.at[part], weight_sem.at[i, c])
             )
 
-    table = slot_table(ids_ref[...])
+    for copy in small[:2]:
+        copy.wait()
+    table = slot_table(ids[...])
     dispatch[...] = dispatch_weights(table)
-    high, low = combine_weights(table, ids_ref[...], gates_ref[...])
+    high, low = combine_weights(table, ids[...], gates[...])
     mixing_ref[:TALL, :] = high
     mixing_ref[TALL:, :] = low
 
-    for copy in small:
+    for copy in small[2:]:
         copy.wait()
-    waiting = list(o_copies)
     for group in range(GROUPS):
-        key_copies[group].wait()
-        value_copies[group].wait()
-        for copy in waiting[:O_STARTS]:
-            copy.start()
-        waiting = waiting[O_STARTS:]
-        attend_group(group, lengths_ref, queries, new_keys, new_values, keys, values, attended)
+        if group % 2 == 0:
+            for g in (group, group + 1):
+                key_copies[g].wait()
+                value_copies[g].wait()
+            for copy in (o_copies, (), weight_copies, ())[group]:
+                copy.start()
+        attend_group(group, lengths, queries, new_keys, new_values, keys, values, attended)
 
     total = hidden[...].astype(F32)
-    waiting = list(weight_copies)
     for c in range(O_CHUNKS):
         o_copies[c].wait()
-        for copy in waiting[:W_STARTS]:
-            copy.start()
-        waiting = waiting[W_STARTS:]
         part = slice(c * O_DEPTH, (c + 1) * O_DEPTH)
         total = total + dot(attended[:, part].astype(BF16), o_weight[part, :])
     after = total.astype(BF16)
     after_ref[...] = after
     after = after.astype(F32)
     mean = jnp.mean(after * after, axis=1, keepdims=True)
-    normed = (after * lax.rsqrt(mean + 1e-6) * gain_ref[...]).astype(BF16)
+    normed = (after * lax.rsqrt(mean + 1e-6) * gain[...]).astype(BF16)
     stacked = jnp.concatenate(
         [normed[:, q * CHUNK_COLS : (q + 1) * CHUNK_COLS] for q in range(BLOCKS)], axis=0
     )
@@ -269,7 +274,6 @@
     o_weight,
     w_gate,
     w_up,
-    w_down,
 ):
     cache = (ROWS_DEV * LMAX, KV_HEADS * HEAD_DIM)
     return pl.pallas_call(
@@ -280,11 +284,14 @@
             pltpu.VMEM((2 * TALL, LINES), BF16),
             pltpu.VMEM((D, FF), BF16),
             pltpu.VMEM((D, FF), BF16),
-            pltpu.VMEM((FF, D), BF16),
         ),
-        in_specs=[SMEM] + [VMEM] * 3 + [HBM] * 10,
-        out_specs=(VMEM,) * 6,
+        in_specs=[HBM] * 13,
+        out_specs=(VMEM,) * 5,
         scratch_shapes=[
+            pltpu.SMEM((ROWS_DEV,), jnp.int32),
+            pltpu.VMEM((TOP, ROWS_DEV), jnp.int32),
+            pltpu.VMEM((TOP, ROWS_DEV), F32),
+            pltpu.VMEM((1, D), F32),
             pltpu.VMEM((ROWS_DEV, D), BF16),
             pltpu.VMEM((ROWS_DEV, D), BF16),
             pltpu.VMEM((ROWS_DEV, KV_HEADS * HEAD_DIM), BF16),
@@ -294,13 +301,13 @@
             pltpu.VMEM((D, D), BF16),
             pltpu.VMEM((ROWS_DEV, D), F32),
             pltpu.VMEM((LINES, TALL), BF16),
-            pltpu.SemaphoreType.DMA((4,)),
+            pltpu.SemaphoreType.DMA((8,)),
             pltpu.SemaphoreType.DMA((GROUPS,)),
             pltpu.SemaphoreType.DMA((GROUPS,)),
             pltpu.SemaphoreType.DMA((O_CHUNKS,)),
             pltpu.SemaphoreType.DMA((3, WEIGHT_PARTS)),
         ],
-        compiler_params=pltpu.CompilerParams(vmem_limit_bytes=50 * MIB),
+        compiler_params=pltpu.CompilerParams(vmem_limit_bytes=53 * MIB),
         cost_estimate=pl.CostEstimate(
             flops=2 * ROWS_DEV * D * D, bytes_accessed=16 * MIB, transcendentals=0
         ),
@@ -319,7 +326,6 @@
         o_weight,
         w_gate,
         w_up,
-        w_down,
     )
 
 
@@ -442,9 +448,8 @@
         o_weight,
         w_gate.reshape(D, FF),
         w_up.reshape(D, FF),
-        w_down.reshape(FF, D),
-    )
-    made = expert_part(exchange(outgoing), *weights)
+    )
+    made = expert_part(exchange(outgoing), *weights, w_down.reshape(FF, D))
     return combine(exchange(made), mixing, after)
 
 

time: 93 us -> 90.1 us (0.969)
  Pallas kernels: 17.9 us -> 15.2 us
    pallas_call x1, Pallas kernels: 10.4 us -> 7.61 us  [attention_part(): pl.pallas_call(attention_kernel, out_shape=(pltpu.VMEM((ROWS_DEV, D), BF1...]
where the time goes in v2:
time: 90.1 us; the launch traced here: 90 us
  blocking collectives  74.8 us (83%)
  Pallas kernels  15.2 us (17%)
    all_to_all x2, blocking collectives, exchange(): lax.all_to_all(array.reshape(EXPERTS, CHUNK_ROWS, CHUNK_COLS), ('sec', 'd...  74.8 us
    pallas_call x1, Pallas kernels, attention_part(): pl.pallas_call(attention_kernel, out_shape=(pltpu.VMEM((ROWS_DEV, D), BF1...  7.61 us
    pallas_call x1, Pallas kernels, expert_part(): pl.pallas_call(expert_kernel, out_shape=pltpu.VMEM((LINES, CHUNK_COLS), B...  6.18 us

profile of v2, /device:TPU:5, one launch (start us, length us, event | category | flops | bytes accessed | tf_op | source)
XLA Modules:
  0.0 90.0 jit_solution(13058219293733520027)
XLA Ops:
  0.0 7.6 %attend.1 = (bf16[32,2048]{1,0:T(8,128)(2,1)S(1)}, bf16[2048,512]{1,0:T(8,128)(2,1)S(1)}, bf16[256,2048]{1,0:T(8,128)(2,1)S(1)}, bf16[2048,768]{1,0:T(8,128)(2,1)S(1)}, bf16[2048,768]{1,0:T(8,128)(2,1)S(1)}) custom-call(s32[32]{0:T(128)} %lengths_hbm.1, s32[8,32]{1,0:T(8,128)} %bitcast.22, f32[8,32]{1,0:T(8,128)} %bitcast.23, f32[1,2048]{1,0:T(1,128)} %bitcast.21, ...), custom_call_target="tpu_custom_call" | custom-call | flops 268435456 | bytes 16777216 | tf_op jit(solution)/shard_map/attend/pallas_call | solution.py:279
  7.6 0.0 copy-start
  7.6 39.9 %all_to_all.10 = bf16[128,16,512]{2,1,0:T(8,128)(2,1)S(1)} all-to-all(bf16[128,16,512]{2,1,0:T(8,128)(2,1)S(1)} %bitcast.13), channel_id=1, replica_groups=mesh['sec'=2,'dev'=64] {'sec','dev'}, dimensions={0} | all-to-all | bytes 4194304 | tf_op jit(solution)/shard_map/all_to_all | solution.py:412
  47.5 0.0 copy-done
  47.5 6.2 %experts.1 = bf16[2048,512]{1,0:T(8,128)(2,1)S(1)} custom-call(bf16[2048,512]{1,0:T(8,128)(2,1)S(1)} %bitcast.14, bf16[2048,768]{1,0:T(8,128)(2,1)S(1)} %get-tuple-element.11.gate_ref, bf16[2048,768]{1,0:T(8,128)(2,1)S(1)} %get-tuple-element.12.up_ref, bf16[768,2048]{1,0:T(8,128)(2,1)S(1)} %bitcast.16), custom_call_target="tpu_custom_call" | custom-call | flops 4831838208 | bytes 12582912 | tf_op jit(solution)/shard_map/experts/pallas_call | solution.py:373
  53.7 34.9 %all_to_all.11 = bf16[128,16,512]{2,1,0:T(8,128)(2,1)S(1)} all-to-all(bf16[128,16,512]{2,1,0:T(8,128)(2,1)S(1)} %bitcast.15), channel_id=1, replica_groups=mesh['sec'=2,'dev'=64] {'sec','dev'}, dimensions={0} | all-to-all | bytes 4194304 | tf_op jit(solution)/shard_map/all_to_all | solution.py:412
  88.6 1.4 %combine.1 = bf16[32,2048]{1,0:T(8,128)(2,1)} custom-call(bf16[2048,512]{1,0:T(8,128)(2,1)S(1)} %bitcast.12, bf16[256,2048]{1,0:T(8,128)(2,1)S(1)} %get-tuple-element.13.mixing_ref, bf16[32,2048]{1,0:T(8,128)(2,1)S(1)} %get-tuple-element.14.after_ref), custom_call_target="tpu_custom_call" | custom-call | flops 536870912 | bytes 4194304 | tf_op jit(solution)/shard_map/combine/pallas_call | solution.py:398
Async XLA Ops:
  7.6 39.9 %copy-start = (bf16[1,768,2048]{2,1,0:T(8,128)(2,1)S(1)}, bf16[1,768,2048]{2,1,0:T(8,128)(2,1)}, u32[]{:S(2)}) copy-start(bf16[1,768,2048]{2,1,0:T(8,128)(2,1)} %param.27) | copy-start | bytes 9437188

commit v3 on v2

--- a/solution.py
+++ b/solution.py
@@ -20,11 +20,8 @@
 EXPERTS = 128
 
 SLOTS = MOST * ROWS_DEV // MICRO
-CHUNK_ROWS = 16
-CHUNK_COLS = SLOTS * D // CHUNK_ROWS
-BLOCKS = CHUNK_ROWS // SLOTS
-LINES = EXPERTS * CHUNK_ROWS
-TALL = BLOCKS * ROWS_DEV
+LINES = EXPERTS * SLOTS
+COPIES = EXPERTS // ROWS_DEV
 
 SUB = 8
 GROUPS = ROWS_DEV // SUB
@@ -33,10 +30,7 @@
 WEIGHT_PARTS = 4
 FF_CHUNK = 256
 
-SHUFFLE = 256
-SOURCES = SHUFFLE // CHUNK_ROWS
-BAND = SOURCES * SLOTS
-SHUFFLES = LINES // SHUFFLE
+OUT_CHUNK = 512
 
 MIB = 2**20
 F32 = jnp.float32
@@ -55,19 +49,20 @@
 
 
 def tile_lanes(array):
-    return jnp.concatenate([array] * BLOCKS, axis=1)
+    return jnp.concatenate([array] * COPIES, axis=1)
 
 
 def slot_table(ids):
     ids = tile_lanes(ids)
-    expert = iota((EXPERTS, TALL), 0)
-    named = jnp.zeros((EXPERTS, TALL), F32)
+    square = (EXPERTS, EXPERTS)
+    expert = iota(square, 0)
+    named = jnp.zeros(square, F32)
     for k in range(TOP):
         named = jnp.where(ids[k : k + 1, :] == expert, 1.0, named)
-    first, second = iota((TALL, TALL), 0), iota((TALL, TALL), 1)
+    first, second = iota(square, 0), iota(square, 1)
     before = jnp.where((first // MICRO == second // MICRO) & (first < second), 1.0, 0.0)
     earlier = dot(named.astype(BF16), before.astype(BF16))
-    micro = (iota((EXPERTS, TALL), 1) % ROWS_DEV) // MICRO
+    micro = (iota(square, 1) % ROWS_DEV) // MICRO
     return named * (earlier + (micro * MOST + 1).astype(F32))
 
 
@@ -113,35 +108,25 @@
 def combine_weights(table, ids, gates):
     ids = tile_lanes(ids)
     gates = tile_lanes(gates)
-    expert = iota((EXPERTS, TALL), 0)
-    gate = jnp.zeros((EXPERTS, TALL), F32)
+    expert = iota((EXPERTS, EXPERTS), 0)
+    gate = jnp.zeros((EXPERTS, EXPERTS), F32)
     for k in range(TOP):
         gate = jnp.where(ids[k : k + 1, :] == expert, gates[k : k + 1, :], gate)
-    gate = jnp.transpose(gate)
+    gate = jnp.transpose(gate)[:ROWS_DEV]
     high = gate.astype(BF16)
     low = (gate - high.astype(F32)).astype(BF16)
-    table = jnp.transpose(table).astype(BF16)
-    lane = iota((EXPERTS, LINES), 1)
-    spread = (lane // CHUNK_ROWS == iota((EXPERTS, LINES), 0)).astype(BF16)
-    lane = iota((TALL, LINES), 1)
-    wanted = jnp.where(
-        (lane // SLOTS) % BLOCKS == iota((TALL, LINES), 0) // ROWS_DEV,
-        (lane % SLOTS + 1).astype(F32),
-        -1.0,
-    )
+    table = jnp.transpose(table)[:ROWS_DEV].astype(BF16)
+    spread = (iota((EXPERTS, LINES), 1) // SLOTS == iota((EXPERTS, LINES), 0)).astype(BF16)
+    wanted = (iota((ROWS_DEV, LINES), 1) % SLOTS + 1).astype(F32)
     live = dot(table, spread) == wanted
     return [jnp.where(live, dot(part, spread), 0.0).astype(BF16) for part in (high, low)]
 
 
 def dispatch_weights(table):
-    line = iota((LINES, EXPERTS), 0)
-    spread = (line // CHUNK_ROWS == iota((LINES, EXPERTS), 1)).astype(BF16)
-    wanted = jnp.where(
-        (line // SLOTS) % BLOCKS == iota((LINES, TALL), 1) // ROWS_DEV,
-        (line % SLOTS + 1).astype(F32),
-        -1.0,
-    )
-    return jnp.where(dot(spread, table.astype(BF16)) == wanted, 1.0, 0.0).astype(BF16)
+    spread = (iota((LINES, EXPERTS), 0) // SLOTS == iota((LINES, EXPERTS), 1)).astype(BF16)
+    wanted = (iota((LINES, EXPERTS), 0) % SLOTS + 1).astype(F32)
+    full = jnp.where(dot(spread, table.astype(BF16)) == wanted, 1.0, 0.0)
+    return full[:, :ROWS_DEV].astype(BF16)
 
 
 def attention_kernel(
@@ -228,9 +213,11 @@
     table = slot_table(ids[...])
     dispatch[...] = dispatch_weights(table)
     high, low = combine_weights(table, ids[...], gates[...])
-    mixing_ref[:TALL, :] = high
-    mixing_ref[TALL:, :] = low
-
+    mixing_ref[:ROWS_DEV, :] = high
+    mixing_ref[ROWS_DEV:, :] = low
+
+    for copy in o_copies:
+        copy.start()
     for copy in small[2:]:
         copy.wait()
     for group in range(GROUPS):
@@ -238,7 +225,7 @@
             for g in (group, group + 1):
                 key_copies[g].wait()
                 value_copies[g].wait()
-            for copy in (o_copies, (), weight_copies, ())[group]:
+            for copy in ((), (), weight_copies, ())[group]:
                 copy.start()
         attend_group(group, lengths, queries, new_keys, new_values, keys, values, attended)
 
@@ -252,10 +239,9 @@
     after = after.astype(F32)
     mean = jnp.mean(after * after, axis=1, keepdims=True)
     normed = (after * lax.rsqrt(mean + 1e-6) * gain[...]).astype(BF16)
-    stacked = jnp.concatenate(
-        [normed[:, q * CHUNK_COLS : (q + 1) * CHUNK_COLS] for q in range(BLOCKS)], axis=0
-    )
-    outgoing_ref[...] = dot(dispatch[...], stacked).astype(BF16)
+    for c in range(0, D, OUT_CHUNK):
+        part = dot(dispatch[...], normed[:, c : c + OUT_CHUNK]).astype(BF16)
+        outgoing_ref[:, :, c : c + OUT_CHUNK] = part.reshape(EXPERTS, SLOTS, OUT_CHUNK)
     for copy in weight_copies:
         copy.wait()
 
@@ -280,8 +266,8 @@
         attention_kernel,
         out_shape=(
             pltpu.VMEM((ROWS_DEV, D), BF16),
-            pltpu.VMEM((LINES, CHUNK_COLS), BF16),
-            pltpu.VMEM((2 * TALL, LINES), BF16),
+            pltpu.VMEM((EXPERTS, SLOTS, D), BF16),
+            pltpu.VMEM((2 * ROWS_DEV, LINES), BF16),
             pltpu.VMEM((D, FF), BF16),
             pltpu.VMEM((D, FF), BF16),
         ),
@@ -300,7 +286,7 @@
             pltpu.VMEM(cache, BF16),
             pltpu.VMEM((D, D), BF16),
             pltpu.VMEM((ROWS_DEV, D), F32),
-            pltpu.VMEM((LINES, TALL), BF16),
+            pltpu.VMEM((LINES, ROWS_DEV), BF16),
             pltpu.SemaphoreType.DMA((8,)),
             pltpu.SemaphoreType.DMA((GROUPS,)),
             pltpu.SemaphoreType.DMA((GROUPS,)),
@@ -329,69 +315,38 @@
     )
 
 
-def shuffle_matrix(back):
-    one, other = (1, 0) if back else (0, 1)
-    banded = iota((SHUFFLE, SHUFFLE), one)
-    chunked = iota((SHUFFLE, SHUFFLE), other)
-    same = (
-        (banded // BAND == (chunked // SLOTS) % BLOCKS)
-        & ((banded % BAND) // SLOTS == chunked // CHUNK_ROWS)
-        & (banded % SLOTS == chunked % SLOTS)
-    )
-    return same.astype(F32).astype(BF16)
-
-
 def expert_kernel(received_ref, gate_ref, up_ref, down_ref, out_ref, rows, inner):
-    spread = shuffle_matrix(False)
-    for b in range(SHUFFLES):
-        part = dot(spread, received_ref[b * SHUFFLE : (b + 1) * SHUFFLE, :]).astype(BF16)
-        for q in range(BLOCKS):
-            rows[b * BAND : (b + 1) * BAND, q * CHUNK_COLS : (q + 1) * CHUNK_COLS] = part[
-                q * BAND : (q + 1) * BAND, :
-            ]
+    rows[...] = received_ref[...].reshape(LINES, D)
     for f in range(0, FF, FF_CHUNK):
         gate = dot(rows[...], gate_ref[:, f : f + FF_CHUNK])
         up = dot(rows[...], up_ref[:, f : f + FF_CHUNK])
         inner[:, f : f + FF_CHUNK] = (gate / (1.0 + jnp.exp(-gate)) * up).astype(BF16)
-    for q in range(BLOCKS):
-        cols = slice(q * CHUNK_COLS, (q + 1) * CHUNK_COLS)
-        rows[:, cols] = dot(inner[...], down_ref[:, cols]).astype(BF16)
-    gather = shuffle_matrix(True)
-    for b in range(SHUFFLES):
-        part = jnp.concatenate(
-            [
-                rows[b * BAND : (b + 1) * BAND, q * CHUNK_COLS : (q + 1) * CHUNK_COLS]
-                for q in range(BLOCKS)
-            ],
-            axis=0,
-        )
-        out_ref[b * SHUFFLE : (b + 1) * SHUFFLE, :] = dot(gather, part).astype(BF16)
+    for c in range(0, D, OUT_CHUNK):
+        part = dot(inner[...], down_ref[:, c : c + OUT_CHUNK]).astype(BF16)
+        out_ref[:, :, c : c + OUT_CHUNK] = part.reshape(EXPERTS, SLOTS, OUT_CHUNK)
 
 
 def expert_part(received, w_gate, w_up, w_down):
-    count = EXPERTS * SLOTS
     return pl.pallas_call(
         expert_kernel,
-        out_shape=pltpu.VMEM((LINES, CHUNK_COLS), BF16),
+        out_shape=pltpu.VMEM((EXPERTS, SLOTS, D), BF16),
         in_specs=[VMEM] * 4,
         out_specs=VMEM,
-        scratch_shapes=[pltpu.VMEM((count, D), BF16), pltpu.VMEM((count, FF), BF16)],
+        scratch_shapes=[pltpu.VMEM((LINES, D), BF16), pltpu.VMEM((LINES, FF), BF16)],
         compiler_params=pltpu.CompilerParams(vmem_limit_bytes=32 * MIB),
         cost_estimate=pl.CostEstimate(
-            flops=6 * count * D * FF, bytes_accessed=12 * MIB, transcendentals=0
+            flops=6 * LINES * D * FF, bytes_accessed=12 * MIB, transcendentals=0
         ),
         name="experts",
     )(received, w_gate, w_up, w_down)
 
 
 def combine_kernel(returned_ref, mixing_ref, after_ref, out_ref):
-    mix = dot(mixing_ref[...], returned_ref[...])
-    mix = mix[:TALL] + mix[TALL:]
-    for q in range(BLOCKS):
-        cols = slice(q * CHUNK_COLS, (q + 1) * CHUNK_COLS)
-        out_ref[:, cols] = (
-            after_ref[:, cols].astype(F32) + mix[q * ROWS_DEV : (q + 1) * ROWS_DEV, :]
-        ).astype(BF16)
+    for c in range(0, D, OUT_CHUNK):
+        cols = slice(c, c + OUT_CHUNK)
+        mix = dot(mixing_ref[...], returned_ref[:, :, cols].reshape(LINES, OUT_CHUNK))
+        mix = mix[:ROWS_DEV] + mix[ROWS_DEV:]
+        out_ref[:, cols] = (after_ref[:, cols].astype(F32) + mix).astype(BF16)
 
 
 def combine(returned, mixing, after):
@@ -402,20 +357,14 @@
         out_specs=VMEM,
         compiler_params=pltpu.CompilerParams(vmem_limit_bytes=24 * MIB),
         cost_estimate=pl.CostEstimate(
-            flops=4 * TALL * LINES * CHUNK_COLS, bytes_accessed=4 * MIB, transcendentals=0
+            flops=4 * ROWS_DEV * LINES * D, bytes_accessed=4 * MIB, transcendentals=0
         ),
         name="combine",
     )(returned, mixing, after)
 
 
 def exchange(array):
-    return lax.all_to_all(
-        array.reshape(EXPERTS, CHUNK_ROWS, CHUNK_COLS),
-        ("sec", "dev"),
-        split_axis=0,
-        concat_axis=0,
-        tiled=True,
-    ).reshape(LINES, CHUNK_COLS)
+    return lax.all_to_all(array, ("sec", "dev"), split_axis=0, concat_axis=0, tiled=True)
 
 
 def on_device(

time: 90.1 us -> 88.2 us (0.979)
  Pallas kernels: 15.2 us -> 13.3 us
    pallas_call x1, Pallas kernels: 6.18 us -> 5.07 us  [expert_part(): pl.pallas_call(expert_kernel, out_shape=pltpu.VMEM((EXPERTS, SLOTS, D), B...]
where the time goes in v3:
time: 88.2 us; the launch traced here: 88.1 us
  blocking collectives  74.8 us (85%)
  Pallas kernels  13.3 us (15%)
    all_to_all x2, blocking collectives, exchange(): lax.all_to_all(array, ('sec', 'dev'), split_axis=0, concat_axis=0, tiled=...  74.8 us
    pallas_call x1, Pallas kernels, attention_part(): pl.pallas_call(attention_kernel, out_shape=(pltpu.VMEM((ROWS_DEV, D), BF1...  7.05 us
    pallas_call x1, Pallas kernels, expert_part(): pl.pallas_call(expert_kernel, out_shape=pltpu.VMEM((EXPERTS, SLOTS, D), B...  5.07 us

profile of v3, /device:TPU:5, one launch (start us, length us, event | category | flops | bytes accessed | tf_op | source)
XLA Modules:
  0.0 88.1 jit_solution(170890402572779537)
XLA Ops:
  0.0 7.0 %attend.1 = (bf16[32,2048]{1,0:T(8,128)(2,1)S(1)}, bf16[128,4,2048]{2,1,0:T(4,128)(2,1)S(1)}, bf16[64,512]{1,0:T(8,128)(2,1)S(1)}, bf16[2048,768]{1,0:T(8,128)(2,1)S(1)}, bf16[2048,768]{1,0:T(8,128)(2,1)S(1)}) custom-call(s32[32]{0:T(128)} %lengths_hbm.1, s32[8,32]{1,0:T(8,128)} %bitcast.14, f32[8,32]{1,0:T(8,128)} %bitcast.15, f32[1,2048]{1,0:T(1,128)} %bitcast.13, ...), custom_call_target="tpu_custom_call" | custom-call | flops 268435456 | bytes 16777216 | tf_op jit(solution)/shard_map/attend/pallas_call | solution.py:265
  7.1 0.0 copy-start
  7.1 39.9 %all_to_all.10.received_ref = bf16[128,4,2048]{2,1,0:T(4,128)(2,1)S(1)} all-to-all(bf16[128,4,2048]{2,1,0:T(4,128)(2,1)S(1)} %get-tuple-element.10), channel_id=1, replica_groups=mesh['sec'=2,'dev'=64] {'sec','dev'}, dimensions={0} | all-to-all | bytes 4194304 | tf_op jit(solution)/shard_map/all_to_all | solution.py:367
  47.0 0.0 copy-done
  47.0 5.1 %experts.1 = bf16[128,4,2048]{2,1,0:T(4,128)(2,1)S(1)} custom-call(bf16[128,4,2048]{2,1,0:T(4,128)(2,1)S(1)} %all_to_all.10.received_ref, bf16[2048,768]{1,0:T(8,128)(2,1)S(1)} %get-tuple-element.11.gate_ref, bf16[2048,768]{1,0:T(8,128)(2,1)S(1)} %get-tuple-element.12.up_ref, bf16[768,2048]{1,0:T(8,128)(2,1)S(1)} %bitcast.8), custom_call_target="tpu_custom_call" | custom-call | flops 4831838208 | bytes 12582912 | tf_op jit(solution)/shard_map/experts/pallas_call | solution.py:330
  52.1 34.9 %all_to_all.11.returned_ref = bf16[128,4,2048]{2,1,0:T(4,128)(2,1)S(1)} all-to-all(bf16[128,4,2048]{2,1,0:T(4,128)(2,1)S(1)} %experts.1), channel_id=1, replica_groups=mesh['sec'=2,'dev'=64] {'sec','dev'}, dimensions={0} | all-to-all | bytes 4194304 | tf_op jit(solution)/shard_map/all_to_all | solution.py:367
  86.9 1.2 %combine.1 = bf16[32,2048]{1,0:T(8,128)(2,1)} custom-call(bf16[128,4,2048]{2,1,0:T(4,128)(2,1)S(1)} %all_to_all.11.returned_ref, bf16[64,512]{1,0:T(8,128)(2,1)S(1)} %get-tuple-element.13.mixing_ref, bf16[32,2048]{1,0:T(8,128)(2,1)S(1)} %get-tuple-element.14.after_ref), custom_call_target="tpu_custom_call" | custom-call | flops 134217728 | bytes 4194304 | tf_op jit(solution)/shard_map/combine/pallas_call | solution.py:353
Async XLA Ops:
  7.1 39.9 %copy-start = (bf16[1,768,2048]{2,1,0:T(8,128)(2,1)S(1)}, bf16[1,768,2048]{2,1,0:T(8,128)(2,1)}, u32[]{:S(2)}) copy-start(bf16[1,768,2048]{2,1,0:T(8,128)(2,1)} %param.27) | copy-start | bytes 9437188

commit v4 on v3

--- a/solution.py
+++ b/solution.py
@@ -25,9 +25,10 @@
 
 SUB = 8
 GROUPS = ROWS_DEV // SUB
-O_CHUNKS = 8
+HALVES = 2
+O_CHUNKS = 4
 O_DEPTH = D // O_CHUNKS
-WEIGHT_PARTS = 4
+WEIGHT_PARTS = 1
 FF_CHUNK = 256
 
 OUT_CHUNK = 512
@@ -184,16 +185,17 @@
     for copy in small:
         copy.start()
     key_copies, value_copies, o_copies = [], [], []
-    for group in range(GROUPS):
-        part = pl.ds(group * SUB * LMAX, SUB * LMAX)
+    depth = ROWS_DEV * LMAX // HALVES
+    for half in range(HALVES):
+        part = pl.ds(half * depth, depth)
         key_copies.append(
-            pltpu.make_async_copy(keys_hbm.at[part], keys.at[part], key_sem.at[group])
+            pltpu.make_async_copy(keys_hbm.at[part], keys.at[part], key_sem.at[half])
         )
         value_copies.append(
-            pltpu.make_async_copy(values_hbm.at[part], values.at[part], value_sem.at[group])
+            pltpu.make_async_copy(values_hbm.at[part], values.at[part], value_sem.at[half])
         )
-        key_copies[group].start()
-        value_copies[group].start()
+        key_copies[half].start()
+        value_copies[half].start()
     for c in range(O_CHUNKS):
         part = pl.ds(c * O_DEPTH, O_DEPTH)
         o_copies.append(pltpu.make_async_copy(o_hbm.at[part], o_weight.at[part], o_sem.at[c]))
@@ -221,11 +223,11 @@
     for copy in small[2:]:
         copy.wait()
     for group in range(GROUPS):
-        if group % 2 == 0:
-            for g in (group, group + 1):
-                key_copies[g].wait()
-                value_copies[g].wait()
-            for copy in ((), (), weight_copies, ())[group]:
+        half, later = divmod(group, GROUPS // HALVES)
+        if later == 0:
+            key_copies[half].wait()
+            value_copies[half].wait()
+            for copy in ((), weight_copies)[half]:
                 copy.start()
         attend_group(group, lengths, queries, new_keys, new_values, keys, values, attended)
 
@@ -288,8 +290,8 @@
             pltpu.VMEM((ROWS_DEV, D), F32),
             pltpu.VMEM((LINES, ROWS_DEV), BF16),
             pltpu.SemaphoreType.DMA((8,)),
-            pltpu.SemaphoreType.DMA((GROUPS,)),
-            pltpu.SemaphoreType.DMA((GROUPS,)),
+            pltpu.SemaphoreType.DMA((HALVES,)),
+            pltpu.SemaphoreType.DMA((HALVES,)),
             pltpu.SemaphoreType.DMA((O_CHUNKS,)),
             pltpu.SemaphoreType.DMA((3, WEIGHT_PARTS)),
         ],

time: 88.2 us -> 88 us (level)
  no operation moved by 1% of the time
where the time goes in v4:
time: 88 us; the launch traced here: 87.9 us
  blocking collectives  74.8 us (85%)
  Pallas kernels  13.1 us (15%)
    all_to_all x2, blocking collectives, exchange(): lax.all_to_all(array, ('sec', 'dev'), split_axis=0, concat_axis=0, tiled=...  74.8 us
    pallas_call x1, Pallas kernels, attention_part(): pl.pallas_call(attention_kernel, out_shape=(pltpu.VMEM((ROWS_DEV, D), BF1...  6.84 us
    pallas_call x1, Pallas kernels, expert_part(): pl.pallas_call(expert_kernel, out_shape=pltpu.VMEM((EXPERTS, SLOTS, D), B...  5.07 us

profile of v4, /device:TPU:5, one launch (start us, length us, event | category | flops | bytes accessed | tf_op | source)
XLA Modules:
  0.0 87.9 jit_solution(12550213846850376245)
XLA Ops:
  0.0 6.8 %attend.1 = (bf16[32,2048]{1,0:T(8,128)(2,1)S(1)}, bf16[128,4,2048]{2,1,0:T(4,128)(2,1)S(1)}, bf16[64,512]{1,0:T(8,128)(2,1)S(1)}, bf16[2048,768]{1,0:T(8,128)(2,1)S(1)}, bf16[2048,768]{1,0:T(8,128)(2,1)S(1)}) custom-call(s32[32]{0:T(128)} %lengths_hbm.1, s32[8,32]{1,0:T(8,128)} %bitcast.14, f32[8,32]{1,0:T(8,128)} %bitcast.15, f32[1,2048]{1,0:T(1,128)} %bitcast.13, ...), custom_call_target="tpu_custom_call" | custom-call | flops 268435456 | bytes 16777216 | tf_op jit(solution)/shard_map/attend/pallas_call | solution.py:267
  6.8 0.0 copy-start
  6.9 39.9 %all_to_all.10.received_ref = bf16[128,4,2048]{2,1,0:T(4,128)(2,1)S(1)} all-to-all(bf16[128,4,2048]{2,1,0:T(4,128)(2,1)S(1)} %get-tuple-element.10), channel_id=1, replica_groups=mesh['sec'=2,'dev'=64] {'sec','dev'}, dimensions={0} | all-to-all | bytes 4194304 | tf_op jit(solution)/shard_map/all_to_all | solution.py:369
  46.8 0.0 copy-done
  46.8 5.1 %experts.1 = bf16[128,4,2048]{2,1,0:T(4,128)(2,1)S(1)} custom-call(bf16[128,4,2048]{2,1,0:T(4,128)(2,1)S(1)} %all_to_all.10.received_ref, bf16[2048,768]{1,0:T(8,128)(2,1)S(1)} %get-tuple-element.11.gate_ref, bf16[2048,768]{1,0:T(8,128)(2,1)S(1)} %get-tuple-element.12.up_ref, bf16[768,2048]{1,0:T(8,128)(2,1)S(1)} %bitcast.8), custom_call_target="tpu_custom_call" | custom-call | flops 4831838208 | bytes 12582912 | tf_op jit(solution)/shard_map/experts/pallas_call | solution.py:332
  51.8 34.9 %all_to_all.11.returned_ref = bf16[128,4,2048]{2,1,0:T(4,128)(2,1)S(1)} all-to-all(bf16[128,4,2048]{2,1,0:T(4,128)(2,1)S(1)} %experts.1), channel_id=1, replica_groups=mesh['sec'=2,'dev'=64] {'sec','dev'}, dimensions={0} | all-to-all | bytes 4194304 | tf_op jit(solution)/shard_map/all_to_all | solution.py:369
  86.7 1.2 %combine.1 = bf16[32,2048]{1,0:T(8,128)(2,1)} custom-call(bf16[128,4,2048]{2,1,0:T(4,128)(2,1)S(1)} %all_to_all.11.returned_ref, bf16[64,512]{1,0:T(8,128)(2,1)S(1)} %get-tuple-element.13.mixing_ref, bf16[32,2048]{1,0:T(8,128)(2,1)S(1)} %get-tuple-element.14.after_ref), custom_call_target="tpu_custom_call" | custom-call | flops 134217728 | bytes 4194304 | tf_op jit(solution)/shard_map/combine/pallas_call | solution.py:355
Async XLA Ops:
  6.8 39.9 %copy-start = (bf16[1,768,2048]{2,1,0:T(8,128)(2,1)S(1)}, bf16[1,768,2048]{2,1,0:T(8,128)(2,1)}, u32[]{:S(2)}) copy-start(bf16[1,768,2048]{2,1,0:T(8,128)(2,1)} %param.27) | copy-start | bytes 9437188

commit v5 on v4

--- a/solution.py
+++ b/solution.py
@@ -30,6 +30,7 @@
 O_DEPTH = D // O_CHUNKS
 WEIGHT_PARTS = 1
 FF_CHUNK = 256
+EXPERT_PARTS = 2
 
 OUT_CHUNK = 512
 
@@ -318,14 +319,19 @@
 
 
 def expert_kernel(received_ref, gate_ref, up_ref, down_ref, out_ref, rows, inner):
-    rows[...] = received_ref[...].reshape(LINES, D)
-    for f in range(0, FF, FF_CHUNK):
-        gate = dot(rows[...], gate_ref[:, f : f + FF_CHUNK])
-        up = dot(rows[...], up_ref[:, f : f + FF_CHUNK])
-        inner[:, f : f + FF_CHUNK] = (gate / (1.0 + jnp.exp(-gate)) * up).astype(BF16)
-    for c in range(0, D, OUT_CHUNK):
-        part = dot(inner[...], down_ref[:, c : c + OUT_CHUNK]).astype(BF16)
-        out_ref[:, :, c : c + OUT_CHUNK] = part.reshape(EXPERTS, SLOTS, OUT_CHUNK)
+    lines = LINES // EXPERT_PARTS
+    sources = EXPERTS // EXPERT_PARTS
+    for p in range(EXPERT_PARTS):
+        mine = slice(p * lines, (p + 1) * lines)
+        there = slice(p * sources, (p + 1) * sources)
+        rows[mine, :] = received_ref[there, :, :].reshape(lines, D)
+        for f in range(0, FF, FF_CHUNK):
+            gate = dot(rows[mine, :], gate_ref[:, f : f + FF_CHUNK])
+            up = dot(rows[mine, :], up_ref[:, f : f + FF_CHUNK])
+            inner[mine, f : f + FF_CHUNK] = (gate / (1.0 + jnp.exp(-gate)) * up).astype(BF16)
+        for c in range(0, D, OUT_CHUNK):
+            part = dot(inner[mine, :], down_ref[:, c : c + OUT_CHUNK]).astype(BF16)
+            out_ref[there, :, c : c + OUT_CHUNK] = part.reshape(sources, SLOTS, OUT_CHUNK)
 
 
 def expert_part(received, w_gate, w_up, w_down):
@@ -343,12 +349,20 @@
     )(received, w_gate, w_up, w_down)
 
 
-def combine_kernel(returned_ref, mixing_ref, after_ref, out_ref):
+def combine_kernel(returned_ref, mixing_ref, after_ref, out_hbm, out, sem):
+    copies = []
     for c in range(0, D, OUT_CHUNK):
         cols = slice(c, c + OUT_CHUNK)
         mix = dot(mixing_ref[...], returned_ref[:, :, cols].reshape(LINES, OUT_CHUNK))
         mix = mix[:ROWS_DEV] + mix[ROWS_DEV:]
-        out_ref[:, cols] = (after_ref[:, cols].astype(F32) + mix).astype(BF16)
+        out[:, cols] = (after_ref[:, cols].astype(F32) + mix).astype(BF16)
+        here = pl.ds(c, OUT_CHUNK)
+        copies.append(
+            pltpu.make_async_copy(out.at[:, here], out_hbm.at[:, here], sem.at[c // OUT_CHUNK])
+        )
+        copies[-1].start()
+    for copy in copies:
+        copy.wait()
 
 
 def combine(returned, mixing, after):
@@ -356,7 +370,11 @@
         combine_kernel,
         out_shape=jax.ShapeDtypeStruct((ROWS_DEV, D), BF16),
         in_specs=[VMEM] * 3,
-        out_specs=VMEM,
+        out_specs=HBM,
+        scratch_shapes=[
+            pltpu.VMEM((ROWS_DEV, D), BF16),
+            pltpu.SemaphoreType.DMA((D // OUT_CHUNK,)),
+        ],
         compiler_params=pltpu.CompilerParams(vmem_limit_bytes=24 * MIB),
         cost_estimate=pl.CostEstimate(
             flops=4 * ROWS_DEV * LINES * D, bytes_accessed=4 * MIB, transcendentals=0

time: 88 us -> 88 us (level)
  no operation moved by 1% of the time
where the time goes in v5:
time: 88 us; the launch traced here: 87.9 us
  blocking collectives  74.8 us (85%)
  Pallas kernels  13.1 us (15%)
    all_to_all x2, blocking collectives, exchange(): lax.all_to_all(array, ('sec', 'dev'), split_axis=0, concat_axis=0, tiled=...  74.8 us
    pallas_call x1, Pallas kernels, attention_part(): pl.pallas_call(attention_kernel, out_shape=(pltpu.VMEM((ROWS_DEV, D), BF1...  6.84 us
    pallas_call x1, Pallas kernels, expert_part(): pl.pallas_call(expert_kernel, out_shape=pltpu.VMEM((EXPERTS, SLOTS, D), B...  5.08 us

profile of v5, /device:TPU:5, one launch (start us, length us, event | category | flops | bytes accessed | tf_op | source)
XLA Modules:
  0.0 87.9 jit_solution(17218407688197618998)
XLA Ops:
  0.0 6.8 %attend.1 = (bf16[32,2048]{1,0:T(8,128)(2,1)S(1)}, bf16[128,4,2048]{2,1,0:T(4,128)(2,1)S(1)}, bf16[64,512]{1,0:T(8,128)(2,1)S(1)}, bf16[2048,768]{1,0:T(8,128)(2,1)S(1)}, bf16[2048,768]{1,0:T(8,128)(2,1)S(1)}) custom-call(s32[32]{0:T(128)} %lengths_hbm.1, s32[8,32]{1,0:T(8,128)} %bitcast.14, f32[8,32]{1,0:T(8,128)} %bitcast.15, f32[1,2048]{1,0:T(1,128)} %bitcast.13, ...), custom_call_target="tpu_custom_call" | custom-call | flops 268435456 | bytes 16777216 | tf_op jit(solution)/shard_map/attend/pallas_call | solution.py:268
  6.8 0.0 copy-start
  6.9 39.9 %all_to_all.10.received_ref = bf16[128,4,2048]{2,1,0:T(4,128)(2,1)S(1)} all-to-all(bf16[128,4,2048]{2,1,0:T(4,128)(2,1)S(1)} %get-tuple-element.10), channel_id=1, replica_groups=mesh['sec'=2,'dev'=64] {'sec','dev'}, dimensions={0} | all-to-all | bytes 4194304 | tf_op jit(solution)/shard_map/all_to_all | solution.py:387
  46.8 0.0 copy-done
  46.8 5.1 %experts.1 = bf16[128,4,2048]{2,1,0:T(4,128)(2,1)S(1)} custom-call(bf16[128,4,2048]{2,1,0:T(4,128)(2,1)S(1)} %all_to_all.10.received_ref, bf16[2048,768]{1,0:T(8,128)(2,1)S(1)} %get-tuple-element.11.gate_ref, bf16[2048,768]{1,0:T(8,128)(2,1)S(1)} %get-tuple-element.12.up_ref, bf16[768,2048]{1,0:T(8,128)(2,1)S(1)} %bitcast.8), custom_call_target="tpu_custom_call" | custom-call | flops 4831838208 | bytes 12582912 | tf_op jit(solution)/shard_map/experts/pallas_call | solution.py:338
  51.8 34.9 %all_to_all.11.returned_ref = bf16[128,4,2048]{2,1,0:T(4,128)(2,1)S(1)} all-to-all(bf16[128,4,2048]{2,1,0:T(4,128)(2,1)S(1)} %experts.1), channel_id=1, replica_groups=mesh['sec'=2,'dev'=64] {'sec','dev'}, dimensions={0} | all-to-all | bytes 4194304 | tf_op jit(solution)/shard_map/all_to_all | solution.py:387
  86.7 1.1 %combine.1 = bf16[32,2048]{1,0:T(8,128)(2,1)} custom-call(bf16[128,4,2048]{2,1,0:T(4,128)(2,1)S(1)} %all_to_all.11.returned_ref, bf16[64,512]{1,0:T(8,128)(2,1)S(1)} %get-tuple-element.13.mixing_ref, bf16[32,2048]{1,0:T(8,128)(2,1)S(1)} %get-tuple-element.14.after_ref), custom_call_target="tpu_custom_call" | custom-call | flops 134217728 | bytes 4194304 | tf_op jit(solution)/shard_map/combine/pallas_call | solution.py:369
Async XLA Ops:
  6.8 39.9 %copy-start = (bf16[1,768,2048]{2,1,0:T(8,128)(2,1)S(1)}, bf16[1,768,2048]{2,1,0:T(8,128)(2,1)}, u32[]{:S(2)}) copy-start(bf16[1,768,2048]{2,1,0:T(8,128)(2,1)} %param.27) | copy-start | bytes 9437188

commit v6 on v4

--- a/solution.py
+++ b/solution.py
@@ -31,7 +31,7 @@
 WEIGHT_PARTS = 1
 FF_CHUNK = 256
 
-OUT_CHUNK = 512
+OUT_CHUNK = 2048
 
 MIB = 2**20
 F32 = jnp.float32

time: 88 us -> 88 us (level)
  no operation moved by 1% of the time
where the time goes in v6:
time: 88 us; the launch traced here: 87.9 us
  blocking collectives  74.8 us (85%)
  Pallas kernels  13.1 us (15%)
    all_to_all x2, blocking collectives, exchange(): lax.all_to_all(array, ('sec', 'dev'), split_axis=0, concat_axis=0, tiled=...  74.8 us
    pallas_call x1, Pallas kernels, attention_part(): pl.pallas_call(attention_kernel, out_shape=(pltpu.VMEM((ROWS_DEV, D), BF1...  6.84 us
    pallas_call x1, Pallas kernels, expert_part(): pl.pallas_call(expert_kernel, out_shape=pltpu.VMEM((EXPERTS, SLOTS, D), B...  5.07 us

profile of v6, /device:TPU:5, one launch (start us, length us, event | category | flops | bytes accessed | tf_op | source)
XLA Modules:
  0.0 87.9 jit_solution(14094691482017490390)
XLA Ops:
  0.0 6.8 %attend.1 = (bf16[32,2048]{1,0:T(8,128)(2,1)S(1)}, bf16[128,4,2048]{2,1,0:T(4,128)(2,1)S(1)}, bf16[64,512]{1,0:T(8,128)(2,1)S(1)}, bf16[2048,768]{1,0:T(8,128)(2,1)S(1)}, bf16[2048,768]{1,0:T(8,128)(2,1)S(1)}) custom-call(s32[32]{0:T(128)} %lengths_hbm.1, s32[8,32]{1,0:T(8,128)} %bitcast.14, f32[8,32]{1,0:T(8,128)} %bitcast.15, f32[1,2048]{1,0:T(1,128)} %bitcast.13, ...), custom_call_target="tpu_custom_call" | custom-call | flops 268435456 | bytes 16777216 | tf_op jit(solution)/shard_map/attend/pallas_call | solution.py:267
  6.8 0.0 copy-start
  6.9 39.9 %all_to_all.10.received_ref = bf16[128,4,2048]{2,1,0:T(4,128)(2,1)S(1)} all-to-all(bf16[128,4,2048]{2,1,0:T(4,128)(2,1)S(1)} %get-tuple-element.10), channel_id=1, replica_groups=mesh['sec'=2,'dev'=64] {'sec','dev'}, dimensions={0} | all-to-all | bytes 4194304 | tf_op jit(solution)/shard_map/all_to_all | solution.py:369
  46.8 0.0 copy-done
  46.8 5.1 %experts.1 = bf16[128,4,2048]{2,1,0:T(4,128)(2,1)S(1)} custom-call(bf16[128,4,2048]{2,1,0:T(4,128)(2,1)S(1)} %all_to_all.10.received_ref, bf16[2048,768]{1,0:T(8,128)(2,1)S(1)} %get-tuple-element.11.gate_ref, bf16[2048,768]{1,0:T(8,128)(2,1)S(1)} %get-tuple-element.12.up_ref, bf16[768,2048]{1,0:T(8,128)(2,1)S(1)} %bitcast.8), custom_call_target="tpu_custom_call" | custom-call | flops 4831838208 | bytes 12582912 | tf_op jit(solution)/shard_map/experts/pallas_call | solution.py:332
  51.8 34.9 %all_to_all.11.returned_ref = bf16[128,4,2048]{2,1,0:T(4,128)(2,1)S(1)} all-to-all(bf16[128,4,2048]{2,1,0:T(4,128)(2,1)S(1)} %experts.1), channel_id=1, replica_groups=mesh['sec'=2,'dev'=64] {'sec','dev'}, dimensions={0} | all-to-all | bytes 4194304 | tf_op jit(solution)/shard_map/all_to_all | solution.py:369
  86.7 1.2 %combine.1 = bf16[32,2048]{1,0:T(8,128)(2,1)} custom-call(bf16[128,4,2048]{2,1,0:T(4,128)(2,1)S(1)} %all_to_all.11.returned_ref, bf16[64,512]{1,0:T(8,128)(2,1)S(1)} %get-tuple-element.13.mixing_ref, bf16[32,2048]{1,0:T(8,128)(2,1)S(1)} %get-tuple-element.14.after_ref), custom_call_target="tpu_custom_call" | custom-call | flops 134217728 | bytes 4194304 | tf_op jit(solution)/shard_map/combine/pallas_call | solution.py:355
Async XLA Ops:
  6.8 39.9 %copy-start = (bf16[1,768,2048]{2,1,0:T(8,128)(2,1)S(1)}, bf16[1,768,2048]{2,1,0:T(8,128)(2,1)}, u32[]{:S(2)}) copy-start(bf16[1,768,2048]{2,1,0:T(8,128)(2,1)} %param.27) | copy-start | bytes 9437188
